TPU v7x, 32 devices: a whole 2x2x4 slice. The times are simulated.
32 devices in a mesh: blk: 8 (over z, core), rep: 4 (over y, x).
Axes of the slice: x: 2, y: 2, z: 4, core: 2. Of those that a mesh axis runs over, the one named last changes fastest.
Arguments:
- features: bfloat16 [24576, 256], P(('blk', 'rep')), may hold values from -6 to 6
- grad_out: bfloat16 [24576, 256], P(('blk', 'rep')), may hold values from -6 to 6
- weight: bfloat16 [256, 256], replicated, may hold values from -0.375 to 0.375
- edge_tiles: bfloat16 [8, 4, 24, 2, 128, 128], P('blk', 'rep'), may hold values from 0 to 0.083984375
- tile_cols: int32 [8, 4, 24, 2], P('blk', 'rep'), may hold values from 0 to 47
- tile_live: int32 [8, 4, 24, 2], P('blk', 'rep'), may hold values 0 or 1
Outputs:
- activations: bfloat16 [24576, 256], P(('blk', 'rep'))
- grad_features: bfloat16 [24576, 256], P(('blk', 'rep'))
- grad_weight: float32 [256, 256], replicated
All inputs are finite; a program needn't handle non-finite values. No bound on the sum of `tile_live` on one device may be relied on, other than what follows from the above.
Results may differ from a plain program's by a relative error of at most 0.014.
Values may be sent and summed in bfloat16 or wider, within the bound.
A program may use at most 128 MiB of HBM per device.

v0:
```python
import math

import jax
import jax.numpy as jnp
from jax import lax
from jax.sharding import PartitionSpec as P


def silu_slope(values):
    sigmoid_val = jax.nn.sigmoid(values)
    return sigmoid_val * (1.0 + values * (1.0 - sigmoid_val))


def per_device(features, grad_out, weight, edge_tiles, tile_cols, tile_live):
    row_count, feat_width = features.shape
    tile_side = edge_tiles.shape[-1]
    panel_tiles = edge_tiles[0, 0] * tile_live[0, 0][..., None, None].astype(edge_tiles.dtype)
    panel_cols = tile_cols[0, 0]
    block_count = panel_tiles.shape[0]
    slot_width = panel_tiles.shape[1]
    projected = jnp.dot(features, weight, preferred_element_type=jnp.float32).astype(jnp.bfloat16)
    slice_feats = lax.all_gather(projected, "blk", axis=0, tiled=True)
    slice_blocks = slice_feats.reshape(-1, tile_side, feat_width)
    picked = slice_blocks[panel_cols]
    partial_value = jnp.einsum(
        "ptij,ptjf->pif", panel_tiles, picked, preferred_element_type=jnp.float32
    )
    partial_value = partial_value.reshape(block_count * tile_side, feat_width)
    own_pre = lax.psum_scatter(
        partial_value.astype(jnp.bfloat16), "rep", scatter_dimension=0, tiled=True
    ).astype(jnp.float32)
    activations = jax.nn.silu(own_pre).astype(jnp.bfloat16)
    own_grad = (grad_out.astype(jnp.float32) * silu_slope(own_pre)).astype(jnp.bfloat16)
    grad_panel = lax.all_gather(own_grad, "rep", axis=0, tiled=True)
    grad_blocks = grad_panel.reshape(block_count, tile_side, feat_width)
    slice_count = slice_blocks.shape[0]
    slice_term = jnp.zeros((slice_count, tile_side, feat_width), jnp.float32)
    for slot in range(slot_width):
        products = jnp.einsum(
            "pij,pif->pjf", panel_tiles[:, slot], grad_blocks, preferred_element_type=jnp.float32
        )
        slice_term = slice_term + jax.ops.segment_sum(
            products, panel_cols[:, slot], num_segments=slice_count
        )
    slice_term = slice_term.reshape(slice_count * tile_side, feat_width)
    own_grad_proj = lax.psum_scatter(
        slice_term.astype(jnp.bfloat16), "blk", scatter_dimension=0, tiled=True
    )
    grad_features = jnp.dot(own_grad_proj, weight.T, preferred_element_type=jnp.float32).astype(
        jnp.bfloat16
    )
    weight_part = jnp.dot(features.T, own_grad_proj, preferred_element_type=jnp.float32)
    total_nodes = row_count * lax.axis_size("blk") * lax.axis_size("rep")
    grad_weight = lax.psum(weight_part, ("blk", "rep")) * (1.0 / math.sqrt(total_nodes))
    return (activations, grad_features, grad_weight)


def solution(mesh):
    placed = (
        P(("blk", "rep"), None),
        P(("blk", "rep"), None),
        P(),
        P("blk", "rep", None, None, None, None),
        P("blk", "rep", None, None),
        P("blk", "rep", None, None),
    )
    return jax.shard_map(
        per_device,
        mesh=mesh,
        in_specs=placed,
        out_specs=(P(("blk", "rep"), None), P(("blk", "rep"), None), P()),
        check_vma=False,
    )
```

profile of v0, /device:TPU:0, one launch (start us, length us, event | category | flops | bytes accessed | tf_op | source)
XLA Modules:
  0.0 338.8 jit_solution(16804968818741668282)
XLA Ops:
  7.2 0.0 copy-start
  7.2 0.0 copy-start.7
  7.2 0.0 all-gather.3.cloned.1.call-start
  7.2 0.9 copy-done
  8.2 1.9 convolution_convert_fusion.1
  10.1 0.0 all-gather.3.cloned.1.call-update
  10.1 0.0 reduce-scatter.3.cloned.1.call-start
  10.1 0.7 compare_select_fusion
  10.8 0.1 copy.14
  10.9 0.1 reshape.56
  11.0 1.9 copy.13
  13.0 0.0 copy-done.7
  13.0 0.2 bitcast_multiply_fusion
  13.2 38.1 %all-gather.3.cloned.1.call-done = bf16[6144,256]{1,0:T(8,128)(2,1)} async-done(((bf16[768,256]{1,0:T(8,128)(2,1)}), bf16[6144,256]{1,0:T(8,128)(2,1)}) %all-gather.3.cloned.1.call-update) | async-done | bytes 3145744 | tf_op jit(solution)/shard_map/all_gather | solution.py:22
  51.3 4.4 %gather_fusion = bf16[48,128,256]{2,1,0:T(8,128)(2,1)} fusion(bf16[48,128,256]{2,1,0:T(8,128)(2,1)} %bitcast.42, s32[1024]{0:T(1024)S(1)} %pad_clamp_fusion), kind=kCustom, calls=%fused_computation | custom fusion | bytes 6291648 | tf_op jit(solution)/shard_map/gather | solution.py:24
  55.6 0.0 copy-start.5
  55.6 3.8 %bitcast_convert_fusion = bf16[24,128,256]{2,1,0:T(8,128)(2,1)} fusion(bf16[24,2,128,128]{2,3,0,1:T(8,128)(2,1)S(1)} %bitcast_multiply_fusion, bf16[24,2,128,256]{3,2,1,0:T(8,128)(2,1)} %bitcast.37), kind=kOutput, calls=%fused_computation.4 | convolution fusion | flops 403439616 | bytes 6291456 | tf_op jit(solution)/shard_map/ptij,ptjf->pif/dot_general | solution.py:25
  59.4 0.0 copy-start.6
  59.4 0.0 reduce-scatter.3.cloned.1.call-update
  59.4 0.0 all-gather.5.cloned.1.call-start
  59.5 29.9 %reduce-scatter.3.cloned.1.call-done = bf16[768,256]{1,0:T(8,128)(2,1)} async-done(((bf16[3072,256]{1,0:T(8,128)(2,1)}), bf16[768,256]{1,0:T(8,128)(2,1)}) %reduce-scatter.3.cloned.1.call-update) | async-done | bytes 393232 | tf_op jit(solution)/shard_map/reduce_scatter | solution.py:29
  89.4 0.0 copy-done.5
  89.4 2.2 fusion.11
  91.6 0.0 all-gather.5.cloned.1.call-update
  91.6 0.0 reduce-scatter.5.cloned.1.call-start
  91.7 0.0 copy-done.6
  91.7 31.1 %all-gather.5.cloned.1.call-done = bf16[3072,256]{1,0:T(8,128)(2,1)} async-done(((bf16[768,256]{1,0:T(8,128)(2,1)}), bf16[3072,256]{1,0:T(8,128)(2,1)}) %all-gather.5.cloned.1.call-update) | async-done | bytes 1572880 | tf_op jit(solution)/shard_map/all_gather | solution.py:34
  122.8 0.0 copy-start.3
  122.8 3.7 %fusion.12 = f32[24,128,256]{2,1,0:T(8,128)} fusion(bf16[24,128,256]{2,1,0:T(8,128)(2,1)} %bitcast.40, bf16[24,2,128,128]{2,3,0,1:T(8,128)(2,1)S(1)} %bitcast_multiply_fusion), kind=kOutput, calls=%fused_computation.23 | convolution fusion | flops 201326592 | bytes 5505024 | tf_op jit(solution)/shard_map/pij,pif->pjf/dot_general | solution.py:39
  126.5 0.0 copy-done.3
  126.5 2.3 fusion.13
  128.8 0.0 copy-start.2
  128.8 3.4 %broadcast.20.clone = f32[48,128,256]{2,1,0:T(8,128)} broadcast(f32[]{:T(128)} %constant.3.clone.1), dimensions={} | broadcast | bytes 6291460 | tf_op jit(solution)/shard_map/broadcast.4
  132.2 0.0 copy-done.2
  132.2 8.5 %scatter_fusion = f32[48,128,256]{2,1,0:T(8,128)} fusion(f32[48,128,256]{2,1,0:T(8,128)} %broadcast.20.clone, s32[24]{0:T(128)S(1)} %get-tuple-element.12, f32[24,128,256]{2,1,0:T(8,128)S(1)} %copy-done.2), kind=kCustom, calls=%fused_computation.1 | custom fusion | flops 786432 | bytes 9437280 | tf_op jit(solution)/shard_map/scatter-add | solution.py:42
  140.7 0.0 copy-start.1
  140.7 3.4 %broadcast.20.clone.1 = f32[48,128,256]{2,1,0:T(8,128)} broadcast(f32[]{:T(128)} %constant.3.clone.1), dimensions={} | broadcast | bytes 6291460 | tf_op jit(solution)/shard_map/broadcast.4
  144.2 0.0 copy-done.1
  144.2 8.5 %scatter_fusion.1 = f32[48,128,256]{2,1,0:T(8,128)} fusion(f32[48,128,256]{2,1,0:T(8,128)} %broadcast.20.clone.1, s32[24]{0:T(128)S(1)} %get-tuple-element.11, f32[24,128,256]{2,1,0:T(8,128)S(1)} %copy-done.1), kind=kCustom, calls=%fused_computation.2 | custom fusion | flops 786432 | bytes 9437280 | tf_op jit(solution)/shard_map/scatter-add | solution.py:42
  152.6 7.3 %add_convert_fusion = bf16[48,128,256]{2,1,0:T(8,128)(2,1)} fusion(f32[48,128,256]{2,1,0:T(8,128)} %scatter_fusion, f32[48,128,256]{2,1,0:T(8,128)} %scatter_fusion.1), kind=kLoop, calls=%fused_computation.3 | loop fusion | flops 3145728 | bytes 15728640 | tf_op jit(solution)/shard_map/convert_element_type | solution.py:47
  159.9 0.0 copy-start.4
  159.9 0.0 reduce-scatter.5.cloned.1.call-update
  160.0 0.0 all-reduce.2.cloned.1.call-start
  160.0 40.4 %reduce-scatter.5.cloned.1.call-done = bf16[768,256]{1,0:T(8,128)(2,1)} async-done(((bf16[6144,256]{1,0:T(8,128)(2,1)}), bf16[768,256]{1,0:T(8,128)(2,1)}) %reduce-scatter.5.cloned.1.call-update) | async-done | bytes 393232 | tf_op jit(solution)/shard_map/reduce_scatter | solution.py:46
  200.4 2.0 convolution_bitcast_fusion
  202.4 0.0 all-reduce.2.cloned.1.call-update
  202.4 0.0 copy-done.4
  202.5 2.0 convolution_convert_fusion
  204.5 125.9 %all-reduce.2.cloned.1.call-done = f32[256,256]{0,1:T(8,128)} async-done(((f32[256,256]{0,1:T(8,128)}), f32[256,256]{0,1:T(8,128)}) %all-reduce.2.cloned.1.call-update) | async-done | bytes 262160 | tf_op jit(solution)/shard_map/psum | solution.py:54
  330.4 1.0 broadcast_multiply_fusion
  331.4 0.8 copy.16
  (3 shorter events, 0.0 us)
Async XLA Ops:
  7.2 1.0 copy-start
  7.2 5.8 %copy-start.7 = (s32[1,1,24,2]{2,3,1,0:T(2,128)S(1)}, s32[1,1,24,2]{2,3,1,0:T(2,128)}, u32[]{:S(2)}) copy-start(s32[1,1,24,2]{2,3,1,0:T(2,128)} %param.11) | copy-start | bytes 580
  7.2 44.1 %all-gather.3.cloned.1.call-start = ((), (), s32[]{:S(2)}) async-start(), calls=%async_computation.2 | async-start | bytes 3538944 | tf_op jit(solution)/shard_map/all_gather | solution.py:22
  10.1 79.3 %reduce-scatter.3.cloned.1.call-start = ((), (), s32[]{:S(2)}) async-start(), calls=%async_computation.3 | async-start | bytes 1966080 | tf_op jit(solution)/shard_map/reduce_scatter | solution.py:29
  55.6 33.8 %copy-start.5 = (bf16[768,256]{1,0:T(8,128)(2,1)S(1)}, bf16[768,256]{1,0:T(8,128)(2,1)}, u32[]{:S(2)}) copy-start(bf16[768,256]{1,0:T(8,128)(2,1)} %param.7) | copy-start | bytes 1179652
  59.4 32.3 %copy-start.6 = (s32[1,1,24,2]{2,3,1,0:T(2,128)S(1)}, s32[1,1,24,2]{2,3,1,0:T(2,128)}, u32[]{:S(2)}) copy-start(s32[1,1,24,2]{2,3,1,0:T(2,128)} %param.10) | copy-start | bytes 580
  59.4 63.4 %all-gather.5.cloned.1.call-start = ((), (), s32[]{:S(2)}) async-start(), calls=%async_computation.4 | async-start | bytes 1966080 | tf_op jit(solution)/shard_map/all_gather | solution.py:34
  91.6 108.8 %reduce-scatter.5.cloned.1.call-start = ((), (), s32[]{:S(2)}) async-start(), calls=%async_computation.5 | async-start | bytes 3538944 | tf_op jit(solution)/shard_map/reduce_scatter | solution.py:46
  122.8 3.7 %copy-start.3 = (bf16[3072,256]{1,0:T(8,128)(2,1)S(1)}, bf16[3072,256]{1,0:T(8,128)(2,1)}, u32[]{:S(2)}) copy-start(bf16[3072,256]{1,0:T(8,128)(2,1)} %all-gather.5.cloned.1.call-done) | copy-start | bytes 4718596
  128.8 3.4 %copy-start.2 = (f32[24,128,256]{2,1,0:T(8,128)S(1)}, f32[24,128,256]{2,1,0:T(8,128)}, u32[]{:S(2)}) copy-start(f32[24,128,256]{2,1,0:T(8,128)} %fusion.13) | copy-start | bytes 9437188
  140.7 3.4 %copy-start.1 = (f32[24,128,256]{2,1,0:T(8,128)S(1)}, f32[24,128,256]{2,1,0:T(8,128)}, u32[]{:S(2)}) copy-start(f32[24,128,256]{2,1,0:T(8,128)} %fusion.12) | copy-start | bytes 9437188
  159.9 42.5 %copy-start.4 = (bf16[256,256]{1,0:T(8,128)(2,1)S(1)}, bf16[256,256]{1,0:T(8,128)(2,1)}, u32[]{:S(2)}) copy-start(bf16[256,256]{1,0:T(8,128)(2,1)} %param.8) | copy-start | bytes 393220
  160.0 170.5 %all-reduce.2.cloned.1.call-start = ((), (), s32[]{:S(2)}) async-start(), calls=%async_computation.6 | async-start | bytes 524288 | tf_op jit(solution)/shard_map/psum | solution.py:54
Sparse Core Ops, SparseCore 0:
  10.2 40.9 all-gather.2
  59.6 29.7 reduce-scatter.2
  91.8 30.9 all-gather.4
  160.1 40.2 reduce-scatter.4
  206.3 124.0 all-reduce.1
where the time goes:
time: 339 us
  waiting for transfers between devices  265 us (78%)
  other arithmetic  28.3 us (8%)
  matrix products  15.7 us (5%)
  local copies, waits for them, and re-layouts  15.1 us (4%)
  between operations  13.9 us (4%)
    psum x1, waiting for transfers between devices, per_device(): lax.psum(weight_part, ('blk', 'rep')) * (1.0 / math.sqrt(total_nodes))  126 us
    reduce_scatter x1, waiting for transfers between devices, per_device(): lax.psum_scatter(slice_term.astype(jnp.bfloat16), 'blk', scatter_dimensio...  40.4 us
    all_gather x1, waiting for transfers between devices, per_device(): slice_feats = lax.all_gather(projected, 'blk', axis=0, tiled=True)  38.1 us
    all_gather x1, waiting for transfers between devices, per_device(): grad_panel = lax.all_gather(own_grad, 'rep', axis=0, tiled=True)  31.1 us
    reduce_scatter x1, waiting for transfers between devices, per_device(): lax.psum_scatter(partial_value.astype(jnp.bfloat16), 'rep', scatter_dimen...  29.9 us
    scatter-add x2, other arithmetic, per_device(): jax.ops.segment_sum(products, panel_cols[:, slot], num_segments=slice_count)  17 us
    convert_element_type x1, other arithmetic, per_device(): slice_term.astype(jnp.bfloat16)  7.29 us
    another operation x2, local copies, waits for them, and re-layouts  6.83 us
  transfers between devices with their start and end apart: 5, of which 5 were waited for; matrix products, arithmetic and copies ran while one was open for 1% of the time, Pallas kernels for 0%

commit v1 on v0

v1 whole, which is shorter than its diff:
```python
import functools
import math

import jax
import jax.numpy as jnp
from jax import lax
from jax.experimental import pallas as pl
from jax.experimental.pallas import tpu as pltpu
from jax.sharding import PartitionSpec as P

MESH = pl.DeviceIdType.MESH
BF = jnp.bfloat16
F32 = jnp.float32
SIDE = 128
LANES = 128


def remote(src, dst, send, recv, where):
    return pltpu.make_async_remote_copy(
        src_ref=src, dst_ref=dst, send_sem=send, recv_sem=recv, device_id=where, device_id_type=MESH
    )


def kernel(
    nb, nr, scale,
    feat, gout, weight, tiles, cols, live, chain,
    act, gfeat, gwout,
    gath0, gath1, part, rsr, panel, runs, pair, snd, crl, crr, gp, featt, gloc, a1, a2, gw,
    ag_s, ag_r, rs_s, rs_r, pa_s, pa_r, pr_s, pr_r, ch_s, cl_r, cr_r, a1_s, a1_r, a2_s, a2_r, a3_s, a3_r,
):
    b = lax.axis_index("blk")
    r = lax.axis_index("rep")
    z = b // 2
    c = b % 2
    nz = nb // 2
    halves = feat.shape[1] // LANES
    bpd = feat.shape[0] // SIDE
    slots = tiles.shape[0]
    panel_blocks = nr * bpd
    per = slots // panel_blocks
    slice_blocks = nb * bpd
    gath = (gath0, gath1)
    sibling = b + 1 - 2 * c
    sp = part

    barrier = pltpu.get_barrier_semaphore()
    for k in range(1, nb):
        pl.semaphore_signal(barrier, inc=1, device_id={"blk": (b + k) % nb}, device_id_type=MESH)
    for k in range(1, nr):
        pl.semaphore_signal(barrier, inc=1, device_id={"rep": (r + k) % nr}, device_id_type=MESH)

    def project(h):
        def step(j, carry):
            rows = pl.ds(pl.multiple_of(j * SIDE, SIDE), SIDE)
            val = jnp.dot(feat[rows, :], weight[:, h * LANES:(h + 1) * LANES], preferred_element_type=F32)
            gath[h][b * bpd + j] = val.astype(BF)
            return carry
        lax.fori_loop(0, bpd, step, 0, unroll=2)
        gath[h][slice_blocks] = jnp.zeros((SIDE, LANES), BF)

    def ag_copy(h, way, slot, to):
        piece = gath[h].at[pl.ds(slot * bpd, bpd)]
        return remote(piece, piece, ag_s.at[h, way, slot], ag_r.at[h, slot], {"blk": to})

    def ag_own(h):
        @pl.when(z < nz - 1)
        def _():
            ag_copy(h, 0, b, b + 2).start()

        @pl.when(z > 0)
        def _():
            ag_copy(h, 1, b, b - 2).start()
        ag_copy(h, 2, b, sibling).start()

    def ag_relay(h, k):
        @pl.when(z - k >= 0)
        def _():
            slot = b - 2 * k
            ag_copy(h, 0, slot, sibling).wait_recv()

            @pl.when(z < nz - 1)
            def _():
                ag_copy(h, 0, slot, b + 2).start()
            ag_copy(h, 2, slot, sibling).start()

        @pl.when(z + k < nz)
        def _():
            slot = b + 2 * k
            ag_copy(h, 1, slot, sibling).wait_recv()

            @pl.when(z > 0)
            def _():
                ag_copy(h, 1, slot, b - 2).start()
            ag_copy(h, 2, slot, sibling).start()

    def ag_finish(h):
        for k in range(nz):
            ag_copy(h, 2, 2 * k + 1 - c, sibling).wait_recv()

    def ag_drain(h):
        for k in range(nz):
            slot = 2 * k + c

            @pl.when((k <= z) & (z < nz - 1))
            def _():
                ag_copy(h, 0, slot, sibling).wait_send()

            @pl.when((k >= z) & (z > 0))
            def _():
                ag_copy(h, 1, slot, sibling).wait_send()
            ag_copy(h, 2, slot, sibling).wait_send()

    def rs_copy(h, k):
        peer = (r + k) % nr
        return remote(
            part.at[h, pl.ds(peer * bpd, bpd)], rsr.at[h, r], rs_s.at[h, k], rs_r.at[h, r], {"rep": peer}
        )

    def rs_from(h, k):
        peer = (r + k) % nr
        return remote(
            part.at[h, pl.ds(peer * bpd, bpd)], rsr.at[h, peer], rs_s.at[h, k], rs_r.at[h, peer], {"rep": peer}
        )

    def forward(h):
        def shard(k, carry):
            peer = (r + k) % nr

            def block(j, inner):
                i = peer * bpd + j
                lhs, rhs = [], []
                for t in range(per):
                    s = i * per + t
                    on = live[s]
                    lhs.append(tiles[s])
                    rhs.append(gath[h][cols[s] * on + slice_blocks * (1 - on)])
                val = jnp.dot(
                    jnp.concatenate(lhs, axis=1), jnp.concatenate(rhs, axis=0), preferred_element_type=F32
                )
                part[h, i] = val.astype(BF)
                return inner
            lax.fori_loop(0, bpd, block, 0, unroll=True)

            @pl.when(k < nr)
            def _():
                rs_copy(h, k).start()
            return carry
        lax.fori_loop(1, nr + 1, shard, 0)

    def pa_copy(h, k):
        piece = panel.at[h, pl.ds(r * bpd, bpd)]
        return remote(piece, piece, pa_s.at[h, k], pa_r.at[h, r], {"rep": (r + k) % nr})

    def pa_from(h, k):
        peer = (r + k) % nr
        piece = panel.at[h, pl.ds(peer * bpd, bpd)]
        return remote(piece, piece, pa_s.at[h, k], pa_r.at[h, peer], {"rep": peer})

    def activate(h):
        for k in range(1, nr):
            rs_from(h, k).wait_recv()
        at = slice(h * LANES, (h + 1) * LANES)

        def step(j, carry):
            rows = pl.ds(pl.multiple_of(j * SIDE, SIDE), SIDE)
            val = part[h, r * bpd + j].astype(F32)
            for k in range(1, nr):
                val = val + rsr[h, (r + k) % nr, j].astype(F32)
            sig = jax.nn.sigmoid(val)
            act[rows, at] = (val * sig).astype(BF)
            slope = sig * (1.0 + val * (1.0 - sig))
            panel[h, r * bpd + j] = (gout[rows, at].astype(F32) * slope).astype(BF)
            return carry
        lax.fori_loop(0, bpd, step, 0)
        for k in range(1, nr):
            pa_copy(h, k).start()

    def pr_copy(h, d):
        return remote(
            sp.at[h, pl.ds((2 * d + 1 - c) * bpd, bpd)], pair.at[h, d], pr_s.at[h, d], pr_r.at[h, d],
            {"blk": sibling},
        )

    def backward(h):
        for k in range(1, nr):
            pa_from(h, k).wait_recv()
            rs_copy(h, k).wait_send()

        def step(i, carry):
            wide = jnp.concatenate([tiles[i * per + t] for t in range(per)], axis=1)
            prod = lax.dot_general(
                wide, panel[h, i], (((0,), (0,)), ((), ())), preferred_element_type=F32
            )
            for t in range(per):
                s = i * per + t
                runs[s] = prod[t * SIDE:(t + 1) * SIDE, :] + runs[chain[s]]
            return carry
        lax.fori_loop(0, panel_blocks, step, 0, unroll=2)

        def collect(shard):
            def move(j, carry):
                q = shard * bpd + j
                sp[h, q] = runs[chain[slots + q]].astype(BF)
                return carry
            lax.fori_loop(0, bpd, move, 0, unroll=2)

        for d in reversed(range(nz)):
            collect(2 * d + 1 - c)
            pr_copy(h, d).start()
        for d in range(nz):
            collect(2 * d + c)

    def right_copy(h, d):
        return remote(snd.at[h, d], crl.at[h, d], ch_s.at[h, d], cl_r.at[h, d], {"blk": b + 2})

    def left_copy(h, d):
        return remote(snd.at[h, d], crr.at[h, d], ch_s.at[h, d], cr_r.at[h, d], {"blk": b - 2})

    def merge(h, d, came):
        def step(j, carry):
            val = sp[h, (2 * d + c) * bpd + j].astype(F32) + pair[h, d, j].astype(F32)
            snd[h, d, j] = (val + came[h, d, j].astype(F32)).astype(BF)
            return carry
        lax.fori_loop(0, bpd, step, 0, unroll=2)

    def chain_step(h, t):
        right, left = nz - 1 - t, t

        @pl.when(z < right)
        def _():
            pr_copy(h, right).wait_recv()

            @pl.when(z > 0)
            def _():
                right_copy(h, right).wait_recv()
            merge(h, right, crl)
            right_copy(h, right).start()

        @pl.when(z > left)
        def _():
            pr_copy(h, left).wait_recv()

            @pl.when(z < nz - 1)
            def _():
                left_copy(h, left).wait_recv()
            merge(h, left, crr)
            left_copy(h, left).start()

    def a1_copy(h, k):
        peer = (b + k) % nb
        return remote(gloc.at[h, peer], a1.at[h, b], a1_s.at[h, k], a1_r.at[h, b], {"blk": peer})

    def a1_from(h, k):
        peer = (b + k) % nb
        return remote(gloc.at[h, peer], a1.at[h, peer], a1_s.at[h, k], a1_r.at[h, peer], {"blk": peer})

    def a2_copy(h, k):
        return remote(a2.at[h, r], a2.at[h, r], a2_s.at[h, k], a2_r.at[h, r], {"rep": (r + k) % nr})

    def a2_from(h, k):
        peer = (r + k) % nr
        return remote(a2.at[h, peer], a2.at[h, peer], a2_s.at[h, k], a2_r.at[h, peer], {"rep": peer})

    def a3_copy(h, k):
        return remote(gw.at[h, b], gw.at[h, b], a3_s.at[h, k], a3_r.at[h, b], {"blk": (b + k) % nb})

    def a3_from(h, k):
        peer = (b + k) % nb
        return remote(gw.at[h, peer], gw.at[h, peer], a3_s.at[h, k], a3_r.at[h, peer], {"blk": peer})

    def chain_finish(h):
        pr_copy(h, z).wait_recv()

        @pl.when(z > 0)
        def _():
            right_copy(h, z).wait_recv()

        @pl.when(z < nz - 1)
        def _():
            left_copy(h, z).wait_recv()

        at = slice(h * LANES, (h + 1) * LANES)

        def step(j, carry):
            rows = pl.ds(pl.multiple_of(j * SIDE, SIDE), SIDE)
            val = sp[h, b * bpd + j].astype(F32) + pair[h, z, j].astype(F32)
            val = val + crl[h, z, j].astype(F32) + crr[h, z, j].astype(F32)
            gp[rows, at] = val.astype(BF)
            return carry
        lax.fori_loop(0, bpd, step, 0, unroll=2)
        share = feat.shape[1] // nb
        for p in range(nb):
            val = jnp.dot(featt[p * share:(p + 1) * share, :], gp[:, at], preferred_element_type=F32)
            gloc[h, p] = val.astype(BF)
        for k in range(1, nb):
            a1_copy(h, k).start()

    def reduce_two(h):
        for k in range(1, nb):
            a1_from(h, k).wait_recv()
        val = gloc[h, b].astype(F32)
        for k in range(1, nb):
            val = val + a1[h, (b + k) % nb].astype(F32)
        a2[h, r] = val.astype(BF)
        for k in range(1, nr):
            a2_copy(h, k).start()

    def reduce_three(h):
        for k in range(1, nr):
            a2_from(h, k).wait_recv()
        val = a2[h, 0].astype(F32)
        for k in range(1, nr):
            val = val + a2[h, k].astype(F32)
        gw[h, b] = val.astype(BF)
        for k in range(1, nb):
            a3_copy(h, k).start()

    def reduce_end(h):
        for k in range(1, nb):
            a3_from(h, k).wait_recv()
        share = feat.shape[1] // nb
        for p in range(nb):
            gwout[p * share:(p + 1) * share, h * LANES:(h + 1) * LANES] = gw[h, p].astype(F32) * scale

    def drain(h):
        ag_drain(h)
        for k in range(1, nr):
            pa_copy(h, k).wait_send()
            a2_copy(h, k).wait_send()
        for k in range(1, nb):
            a1_copy(h, k).wait_send()
            a3_copy(h, k).wait_send()
        for d in range(nz):
            pr_copy(h, d).wait_send()

            @pl.when(z != d)
            def _():
                right_copy(h, d).wait_send()

    project(0)
    pl.semaphore_wait(barrier, nb - 1 + nr - 1)
    ag_own(0)
    project(1)
    runs[slots] = jnp.zeros((SIDE, LANES), F32)
    featt[...] = feat[...].T

    @pl.when(z == 0)
    def _():
        crl[...] = jnp.zeros(crl.shape, BF)

    @pl.when(z == nz - 1)
    def _():
        crr[...] = jnp.zeros(crr.shape, BF)

    for k in range(1, nz):
        ag_relay(0, k)
    ag_own(1)
    ag_finish(0)
    forward(0)
    for k in range(1, nz - 1):
        ag_relay(1, k)
    activate(0)
    ag_relay(1, nz - 1)
    ag_finish(1)
    forward(1)
    backward(0)
    chain_step(0, 0)
    activate(1)
    for t in range(1, nz - 1):
        chain_step(0, t)
    backward(1)
    chain_finish(0)
    chain_step(1, 0)
    reduce_two(0)
    for t in range(1, nz - 1):
        chain_step(1, t)
    reduce_three(0)
    chain_finish(1)

    def out_rows(j, carry):
        rows = pl.ds(pl.multiple_of(j * SIDE, SIDE), SIDE)
        val = lax.dot_general(gp[rows, :], weight[...], (((1,), (1,)), ((), ())), preferred_element_type=F32)
        gfeat[rows, :] = val.astype(BF)
        return carry
    lax.fori_loop(0, bpd, out_rows, 0, unroll=2)
    reduce_two(1)
    reduce_end(0)
    reduce_three(1)
    drain(0)
    reduce_end(1)
    drain(1)


def per_device(nb, nr, features, grad_out, weight, edge_tiles, tile_cols, tile_live):
    rows, width = features.shape
    side = edge_tiles.shape[-1]
    bpd = rows // side
    tiles = edge_tiles.reshape(-1, side, side)
    slots = tiles.shape[0]
    cols = tile_cols.reshape(-1)
    live = tile_live.reshape(-1)
    blocks = nb * bpd
    halves = width // LANES
    nz = nb // 2
    share = width // nb
    order = jnp.arange(slots, dtype=jnp.int32)
    keys = jnp.concatenate([cols, jnp.arange(blocks, dtype=jnp.int32)])
    limit = jnp.concatenate([order, jnp.full((blocks,), slots, jnp.int32)])
    hit = (keys[:, None] == cols[None, :]) & (live[None, :] == 1) & (order[None, :] < limit[:, None])
    chain = jnp.max(jnp.where(hit, order[None, :], -1), axis=1)
    chain = jnp.where(chain < 0, slots, chain)

    vm = pl.BlockSpec(memory_space=pltpu.VMEM)
    sm = pl.BlockSpec(memory_space=pltpu.SMEM)
    block = (SIDE, LANES)
    dma = pltpu.SemaphoreType.DMA
    scratch = [
        pltpu.VMEM((blocks + 1,) + block, BF),
        pltpu.VMEM((blocks + 1,) + block, BF),
        pltpu.VMEM((halves, max(blocks, nr * bpd)) + block, BF),
        pltpu.VMEM((halves, nr, bpd) + block, BF),
        pltpu.VMEM((halves, nr * bpd) + block, BF),
        pltpu.VMEM((slots + 1,) + block, F32),
        pltpu.VMEM((halves, nz, bpd) + block, BF),
        pltpu.VMEM((halves, nz, bpd) + block, BF),
        pltpu.VMEM((halves, nz, bpd) + block, BF),
        pltpu.VMEM((halves, nz, bpd) + block, BF),
        pltpu.VMEM((rows, width), BF),
        pltpu.VMEM((width, rows), BF),
        pltpu.VMEM((halves, nb, share, LANES), BF),
        pltpu.VMEM((halves, nb, share, LANES), BF),
        pltpu.VMEM((halves, nr, share, LANES), BF),
        pltpu.VMEM((halves, nb, share, LANES), BF),
        dma((halves, 3, nb)), dma((halves, nb)),
        dma((halves, nr)), dma((halves, nr)),
        dma((halves, nr)), dma((halves, nr)),
        dma((halves, nz)), dma((halves, nz)),
        dma((halves, nz)), dma((halves, nz)), dma((halves, nz)),
        dma((halves, nb)), dma((halves, nb)),
        dma((halves, nr)), dma((halves, nr)),
        dma((halves, nb)), dma((halves, nb)),
    ]
    scale = 1.0 / math.sqrt(rows * nb * nr)
    return pl.pallas_call(
        functools.partial(kernel, nb, nr, scale),
        out_shape=(
            jax.ShapeDtypeStruct((rows, width), BF),
            jax.ShapeDtypeStruct((rows, width), BF),
            jax.ShapeDtypeStruct((width, width), F32),
        ),
        in_specs=[vm, vm, vm, vm, sm, sm, sm],
        out_specs=(vm, vm, vm),
        scratch_shapes=scratch,
        compiler_params=pltpu.CompilerParams(
            collective_id=0, has_side_effects=True, vmem_limit_bytes=61 * 1024 * 1024
        ),
    )(features, grad_out, weight, tiles, cols, live, chain)


def solution(mesh):
    placed = (
        P(("blk", "rep"), None),
        P(("blk", "rep"), None),
        P(),
        P("blk", "rep", None, None, None, None),
        P("blk", "rep", None, None),
        P("blk", "rep", None, None),
    )
    return jax.shard_map(
        functools.partial(per_device, mesh.shape["blk"], mesh.shape["rep"]),
        mesh=mesh,
        in_specs=placed,
        out_specs=(P(("blk", "rep"), None), P(("blk", "rep"), None), P()),
        check_vma=False,
    )
```

time: 339 us -> 126 us (0.37)
  waiting for transfers between devices: 265 us -> 0 us
  Pallas kernels: 0 us -> 118 us
  other arithmetic: 28.3 us -> 1.35 us
  matrix products: 15.7 us -> 0 us
  between operations: 13.9 us -> 0.69 us
  local copies, waits for them, and re-layouts: 15.1 us -> 6 us
    psum x1 -> x0, waiting for transfers between devices: 126 us -> none  [per_device(): lax.psum(weight_part, ('blk', 'rep')) * (1.0 / math.sqrt(total_nodes))]
    pallas_call x0 -> x1, Pallas kernels: none -> 118 us  [per_device(): pl.pallas_call(functools.partial(kernel, nb, nr, scale), out_shape=(jax.S...]
    reduce_scatter x2 -> x0, waiting for transfers between devices: 70.3 us -> none  [the longest x1 40.4 us: per_device(): lax.psum_scatter(slice_term.astype(jnp.bfloat16), 'blk', scatter_dimensio...]
    all_gather x2 -> x0, waiting for transfers between devices: 69.2 us -> none  [the longest x1 38.1 us: per_device(): slice_feats = lax.all_gather(projected, 'blk', axis=0, tiled=True)]
    scatter-add x2 -> x0, other arithmetic: 17 us -> none  [per_device(): jax.ops.segment_sum(products, panel_cols[:, slot], num_segments=slice_count)]
    dot_general x6 -> x0, matrix products: 15.7 us -> none  [the longest x2 6 us: per_device(): jnp.einsum('pij,pif->pjf', panel_tiles[:, slot], grad_blocks, preferred_e...]
    convert_element_type x3 -> x0, other arithmetic: 9.52 us -> none  [the longest x1 7.29 us: per_device(): slice_term.astype(jnp.bfloat16)]
    another operation x2 -> x0, local copies, waits for them, and re-layouts: 6.83 us -> none
  transfers between devices with their start and end apart: 5 -> 0, of which waited for: 5 -> 0; matrix products, arithmetic and copies ran while one was open for 1% -> 0% of each run, Pallas kernels for 0% -> 0%
where the time goes in v1:
time: 126 us
  Pallas kernels  118 us (94%)
  local copies, waits for them, and re-layouts  6 us (5%)
  other arithmetic  1.35 us (1%)
    pallas_call x1, Pallas kernels, per_device(): pl.pallas_call(functools.partial(kernel, nb, nr, scale), out_shape=(jax.S...  118 us
    unnamed x11, local copies, waits for them, and re-layouts  5.81 us

profile of v1, /device:TPU:0, one launch (start us, length us, event | category | flops | bytes accessed | tf_op | source)
XLA Modules:
  0.0 125.8 jit_solution(11432346048430434224)
XLA Ops:
  0.6 0.8 copy.13
  1.4 0.1 reshape.26.cols
  1.5 0.0 copy-start.1
  1.5 0.1 pad_add_fusion
  1.6 0.8 copy.14
  2.3 0.1 reshape.27.live
  2.4 0.0 copy-start.2
  2.5 0.8 select_reduce_fusion
  3.2 0.5 compare_select_fusion.chain
  3.7 0.0 copy-done.1
  3.7 0.0 copy-done.2
  3.7 117.8 %shard_map.85 = (bf16[768,256]{1,0:T(8,128)(2,1)}, bf16[768,256]{1,0:T(8,128)(2,1)}, f32[256,256]{1,0:T(8,128)}) custom-call(bf16[768,256]{1,0:T(8,128)(2,1)} %feat.1, bf16[768,256]{1,0:T(8,128)(2,1)} %gout.1, bf16[256,256]{1,0:T(8,128)(2,1)} %weight.1, bf16[48,128,128]{2,1,0:T(8,128)(2,1)} %bitcast.5, s32[48]{0:T(128)} %copy-done.1, s32[48]{0:T(128)} %copy-done.2, ...), custom_call_target="tpu_custom_call" | custom-call | tf_op jit(solution)/shard_map/pallas_call | solution.py:444
  121.5 0.0 copy-start
  121.5 1.8 %copy.18 = bf16[768,256]{1,0:T(8,128)(2,1)} copy(bf16[768,256]{1,0:T(8,128)(2,1)} %get-tuple-element.6) | data formatting | bytes 786432
  123.3 1.8 %copy.19 = bf16[768,256]{1,0:T(8,128)(2,1)} copy(bf16[768,256]{1,0:T(8,128)(2,1)} %get-tuple-element.7) | data formatting | bytes 786432
  125.1 0.0 copy-done
  125.1 0.7 copy.20
  (2 shorter events, 0.0 us)
Async XLA Ops:
  1.5 2.2 %copy-start.1 = (s32[48]{0:T(128)}, s32[48]{0:T(128)S(1)}, u32[]{:S(2)}) copy-start(s32[48]{0:T(128)S(1)} %reshape.26.cols) | copy-start | bytes 580
  2.4 1.3 %copy-start.2 = (s32[48]{0:T(128)}, s32[48]{0:T(128)S(1)}, u32[]{:S(2)}) copy-start(s32[48]{0:T(128)S(1)} %reshape.27.live) | copy-start | bytes 580
  121.5 3.6 %copy-start = (f32[256,256]{1,0:T(8,128)S(1)}, f32[256,256]{1,0:T(8,128)}, u32[]{:S(2)}) copy-start(f32[256,256]{1,0:T(8,128)} %get-tuple-element.8) | copy-start | bytes 786436

commit v2 on v1

--- a/solution.py
+++ b/solution.py
@@ -25,7 +25,7 @@
     nb, nr, scale,
     feat, gout, weight, tiles, cols, live, chain,
     act, gfeat, gwout,
-    gath0, gath1, part, rsr, panel, runs, pair, snd, crl, crr, gp, featt, gloc, a1, a2, gw,
+    gath0, gath1, part, rsr, panel, runs, pair, snd, crl, crr, gp, featt, turned, gloc, a1, a2, gw,
     ag_s, ag_r, rs_s, rs_r, pa_s, pa_r, pr_s, pr_r, ch_s, cl_r, cr_r, a1_s, a1_r, a2_s, a2_r, a3_s, a3_r,
 ):
     b = lax.axis_index("blk")
@@ -187,15 +187,22 @@
             rs_copy(h, k).wait_send()
 
         def step(i, carry):
-            wide = jnp.concatenate([tiles[i * per + t] for t in range(per)], axis=1)
-            prod = lax.dot_general(
-                wide, panel[h, i], (((0,), (0,)), ((), ())), preferred_element_type=F32
-            )
+            if turned.shape[0] == panel_blocks:
+                prod = jnp.dot(turned[i], panel[h, i], preferred_element_type=F32)
+            else:
+                wide = jnp.concatenate([tiles[i * per + t] for t in range(per)], axis=1)
+                prod = lax.dot_general(
+                    wide, panel[h, i], (((0,), (0,)), ((), ())), preferred_element_type=F32
+                )
             for t in range(per):
-                s = i * per + t
-                runs[s] = prod[t * SIDE:(t + 1) * SIDE, :] + runs[chain[s]]
-            return carry
-        lax.fori_loop(0, panel_blocks, step, 0, unroll=2)
+                runs[i * per + t] = prod[t * SIDE:(t + 1) * SIDE, :]
+            return carry
+        lax.fori_loop(0, panel_blocks, step, 0, unroll=4)
+
+        def link(s, carry):
+            runs[s] = runs[s] + runs[chain[s]]
+            return carry
+        lax.fori_loop(0, slots, link, 0, unroll=2)
 
         def collect(shard):
             def move(j, carry):
@@ -352,7 +359,14 @@
     def _():
         crr[...] = jnp.zeros(crr.shape, BF)
 
-    for k in range(1, nz):
+    ag_relay(0, 1)
+    if turned.shape[0] == panel_blocks:
+        def turn(i, carry):
+            for t in range(per):
+                turned[i, t * SIDE:(t + 1) * SIDE, :] = tiles[i * per + t].T
+            return carry
+        lax.fori_loop(0, panel_blocks, turn, 0, unroll=2)
+    for k in range(2, nz):
         ag_relay(0, k)
     ag_own(1)
     ag_finish(0)
@@ -427,6 +441,7 @@
         pltpu.VMEM((halves, nz, bpd) + block, BF),
         pltpu.VMEM((rows, width), BF),
         pltpu.VMEM((width, rows), BF),
+        pltpu.VMEM((nr * bpd if slots <= 64 else 1, slots // (nr * bpd) * SIDE, SIDE), BF),
         pltpu.VMEM((halves, nb, share, LANES), BF),
         pltpu.VMEM((halves, nb, share, LANES), BF),
         pltpu.VMEM((halves, nr, share, LANES), BF),

time: 126 us -> 124 us (0.984)
  Pallas kernels: 118 us -> 116 us
    pallas_call x1, Pallas kernels: 118 us -> 116 us  [per_device(): pl.pallas_call(functools.partial(kernel, nb, nr, scale), out_shape=(jax.S...]
where the time goes in v2:
time: 124 us
  Pallas kernels  116 us (94%)
  local copies, waits for them, and re-layouts  6 us (5%)
  other arithmetic  1.35 us (1%)
    pallas_call x1, Pallas kernels, per_device(): pl.pallas_call(functools.partial(kernel, nb, nr, scale), out_shape=(jax.S...  116 us
    unnamed x11, local copies, waits for them, and re-layouts  5.81 us

profile of v2, /device:TPU:0, one launch (start us, length us, event | category | flops | bytes accessed | tf_op | source)
XLA Modules:
  0.0 123.9 jit_solution(8165346335794395983)
XLA Ops:
  0.6 0.8 copy.13
  1.4 0.1 reshape.26.cols
  1.5 0.0 copy-start.1
  1.5 0.1 pad_add_fusion
  1.6 0.8 copy.14
  2.3 0.1 reshape.27.live
  2.4 0.0 copy-start.2
  2.5 0.8 select_reduce_fusion
  3.2 0.5 compare_select_fusion.chain
  3.7 0.0 copy-done.1
  3.7 0.0 copy-done.2
  3.7 115.8 %shard_map.85 = (bf16[768,256]{1,0:T(8,128)(2,1)}, bf16[768,256]{1,0:T(8,128)(2,1)}, f32[256,256]{1,0:T(8,128)}) custom-call(bf16[768,256]{1,0:T(8,128)(2,1)} %feat.1, bf16[768,256]{1,0:T(8,128)(2,1)} %gout.1, bf16[256,256]{1,0:T(8,128)(2,1)} %weight.1, bf16[48,128,128]{2,1,0:T(8,128)(2,1)} %bitcast.5, s32[48]{0:T(128)} %copy-done.1, s32[48]{0:T(128)} %copy-done.2, ...), custom_call_target="tpu_custom_call" | custom-call | tf_op jit(solution)/shard_map/pallas_call | solution.py:459
  119.6 0.0 copy-start
  119.6 1.8 %copy.18 = bf16[768,256]{1,0:T(8,128)(2,1)} copy(bf16[768,256]{1,0:T(8,128)(2,1)} %get-tuple-element.6) | data formatting | bytes 786432
  121.4 1.8 %copy.19 = bf16[768,256]{1,0:T(8,128)(2,1)} copy(bf16[768,256]{1,0:T(8,128)(2,1)} %get-tuple-element.7) | data formatting | bytes 786432
  123.2 0.0 copy-done
  123.2 0.7 copy.20
  (2 shorter events, 0.0 us)
Async XLA Ops:
  1.5 2.2 %copy-start.1 = (s32[48]{0:T(128)}, s32[48]{0:T(128)S(1)}, u32[]{:S(2)}) copy-start(s32[48]{0:T(128)S(1)} %reshape.26.cols) | copy-start | bytes 580
  2.4 1.3 %copy-start.2 = (s32[48]{0:T(128)}, s32[48]{0:T(128)S(1)}, u32[]{:S(2)}) copy-start(s32[48]{0:T(128)S(1)} %reshape.27.live) | copy-start | bytes 580
  119.6 3.6 %copy-start = (f32[256,256]{1,0:T(8,128)S(1)}, f32[256,256]{1,0:T(8,128)}, u32[]{:S(2)}) copy-start(f32[256,256]{1,0:T(8,128)} %get-tuple-element.8) | copy-start | bytes 786436
